TPU v7x, 128 devices: a whole 4x4x4 slice. The times are simulated.
128 devices in a mesh: frame: 4 (over y_hi, core), tok: 16 (over x, z), dp: 2 (over y_lo).
Axes of the slice: x: 4, y: 4 (y_hi: 2, y_lo: 2; y = y_hi * 2 + y_lo), z: 4, core: 2. Of those that a mesh axis runs over, the one named last changes fastest.
Arguments:
- queries: bfloat16 [4, 1024, 2048], P('dp', 'tok', 'frame'), may hold values from -200 to 200
- bank: bfloat16 [4, 8, 1024, 4096], P('dp', 'frame', 'tok'), may hold values from -4 to 4
- read_mask: int32 [4, 8], P('dp', 'frame'), may hold values from 0 to 1, as said below
Outputs:
- attended: bfloat16 [4, 1024, 2048], P('dp', 'tok', 'frame')
Inputs may be any that keep to these rules, and one draw needn't show every extreme that they name: `read_mask`: each sample reads between 4 and 8 frames, always its frame 0; in every draw some sample reads all 8 frames and some reads exactly 4.
All inputs are finite; a program needn't handle non-finite values.
Results may differ from a plain program's by a relative error of at most 0.0049.
Values may be sent and summed in bfloat16 or wider, within the bound.
A program may use at most 128 MiB of HBM per device.

v0:
```python
import math

import jax
import jax.numpy as jnp
from jax import lax
from jax.experimental import pallas as pl
from jax.experimental.pallas import tpu as pltpu
from jax.sharding import PartitionSpec as P

MESH = pl.DeviceIdType.MESH
HEAD_DIM = 64
PAIR = 2 * HEAD_DIM
TOK = 64
KEYS_COLS = 2048
MASKED = -1e30
FLOOR = -1e20

ORDER = (0, 4, 12, 1, 3, 16, 20, 5, 28, 15, 24, 2, 8, 7, 13, 6, 9, 11, 17, 19, 21, 31, 23, 29, 18, 14, 25, 27, 22, 30, 10, 26)
SIZES = (4, 4, 4, 4, 4, 4, 4, 4)
STARTS = tuple(sum(SIZES[:i]) for i in range(len(SIZES)))
GROUPS = len(SIZES)
BATCHES = (6,) + (2,) * 13
BATCH_STARTS = tuple(sum(BATCHES[:i]) for i in range(len(BATCHES)))
GROUP_OF = tuple(i for i, size in enumerate(SIZES) for _ in range(size))
NEAR = 7
FLY = 10


def kernel(q_ref, bank_ref, mask_ref, out_ref, q_buf, q_heads, kv, bias, mask_tile, mask_smem, acc, peak, outs,
           q_send, q_recv, kv_send, kv_recv, fwd_send, fwd_recv, mask_send, mask_recv, mask_copy,
           out_send, out_recv, plane_sem, sibling_sem, far_sem):
    frame, tok = lax.axis_index("frame"), lax.axis_index("tok")
    y, core = frame // 2, frame % 2
    x, z = tok // 4, tok % 4
    samp, pair = tok // 8, tok % 8
    sibling = 2 * y + 1 - core
    across = (frame + 2) % 4
    x_mates = [((x + i) % 4) * 4 + z for i in range(1, 4)]
    z_mates = [x * 4 + (z + i) % 4 for i in range(1, 4)]

    def tell(sem, to_frame, to_tok):
        pl.semaphore_signal(sem, inc=1, device_id={"frame": to_frame, "tok": to_tok}, device_id_type=MESH)

    def send(src, dst, send_sem, recv_sem, to_frame, to_tok):
        copy = pltpu.make_async_remote_copy(
            src, dst, send_sem, recv_sem, device_id={"frame": to_frame, "tok": to_tok}, device_id_type=MESH
        )
        copy.start()

    def send_or_keep(src, dst, send_sem, recv_sem, to_frame, to_tok):
        here = (to_frame == frame) & (to_tok == tok)

        @pl.when(here)
        def _():
            pltpu.make_async_copy(src, dst, recv_sem).start()

        @pl.when(jnp.logical_not(here))
        def _():
            send(src, dst, send_sem, recv_sem, to_frame, to_tok)

    def wait_bytes(ref, sem):
        pltpu.make_async_copy(ref, ref, sem).wait()

    def wait_sent(blocks, sem, kept):
        @pl.when(kept)
        def _():
            wait_bytes(blocks.at[pl.ds(0, 7)], sem)

        @pl.when(jnp.logical_not(kept))
        def _():
            wait_bytes(blocks, sem)

    def send_batch(batch):
        for slot in range(BATCH_STARTS[batch], BATCH_STARTS[batch] + BATCHES[batch]):
            code = ORDER[slot]
            dy, dx, dz = code // 16, code // 4 % 4, code % 4
            dx = jnp.where(core == 1, (4 - dx) % 4, dx)
            dz = jnp.where(core == 1, (4 - dz) % 4, dz)
            to_y, to_tok = (y + dy) % 2, (x + dx) % 4 * 4 + (z + dz) % 4
            column = (8 * to_y + to_tok % 8) * PAIR
            arrived = kv_recv.at[GROUP_OF[slot]]
            for part in range(2):
                src = bank_ref.at[to_tok // 8, :, :, pl.ds(pl.multiple_of(part * KEYS_COLS + column, PAIR), PAIR)]
                dst = kv.at[0, slot, part]
                if code == 0:
                    pltpu.make_async_copy(src, dst, arrived).start()
                else:
                    send(src, dst, kv_send.at[batch], arrived, 2 * to_y + core, to_tok)

    def wait_batch_sent(batch):
        sent = BATCHES[batch] - (1 if batch == 0 else 0)
        wait_bytes(kv.at[0, pl.ds(0, sent)], kv_send.at[batch])

    def send_next(batch):
        if batch < len(BATCHES):
            wait_batch_sent(batch - FLY)
            send_batch(batch)

    barrier = pltpu.get_barrier_semaphore()
    tell(barrier, sibling, tok)
    tell(barrier, across, tok)
    for mate in x_mates + z_mates:
        tell(barrier, frame, mate)
    pltpu.make_async_copy(mask_ref, mask_smem, mask_copy).start()
    mask_tile[...] = jnp.zeros_like(mask_tile)
    acc[...] = jnp.zeros_like(acc)
    peak[...] = jnp.full_like(peak, FLOOR)
    wait_bytes(mask_smem, mask_copy)
    for s in range(2):
        for j in range(2):
            flag = (mask_smem[s, j].astype(jnp.float32) - 1.0) * (-MASKED)
            mask_tile[pl.ds(2 * s + j, 1), :] = jnp.full((1, 128), flag, jnp.float32)
    bias[pl.ds(frame, 1)] = mask_tile[...][None]
    pl.semaphore_wait(barrier, 8)

    for mate in x_mates:
        tell(plane_sem, frame, mate)
    send_batch(0)
    pl.semaphore_wait(plane_sem, 3)

    tell(sibling_sem, sibling, tok)
    tell(far_sem, across, tok)
    pl.semaphore_wait(sibling_sem, 1)
    for s in range(2):
        for j in range(4):
            send_or_keep(
                q_ref.at[s, :, pl.ds(j * PAIR, PAIR)], q_buf.at[tok % 8], q_send, q_recv,
                2 * y + tok // 8, 8 * s + 4 * core + j,
            )
    for batch in range(1, NEAR):
        send_batch(batch)
    pl.semaphore_wait(far_sem, 1)
    for batch in range(NEAR, FLY):
        send_batch(batch)
    for i in range(1, 4):
        send(mask_tile, bias.at[frame], mask_send, mask_recv, (frame + i) % 4, tok)
    send_next(FLY)
    wait_bytes(q_buf, q_recv)
    others = bias.at[pl.ds(0, 3)]
    wait_bytes(others, mask_recv)

    queries = q_buf[...].reshape(8 * TOK, PAIR).astype(jnp.float32) * (1.0 / math.sqrt(HEAD_DIM))
    first = lax.broadcasted_iota(jnp.int32, queries.shape, 1) < HEAD_DIM
    q_heads[0] = jnp.where(first, queries, 0.0).astype(jnp.bfloat16)
    q_heads[1] = jnp.where(first, 0.0, queries).astype(jnp.bfloat16)

    def work(half, group, from_core):
        start, size = STARTS[group], SIZES[group]
        keys = kv[half, pl.ds(start, size), 0].reshape(size * 2 * TOK, PAIR)
        values = kv[half, pl.ds(start, size), 1].reshape(size * 2 * TOK, PAIR)
        values_t = values.T
        top = lax.broadcasted_iota(jnp.int32, values_t.shape, 0) < HEAD_DIM
        one = jnp.ones_like(values_t)
        biases = []
        for i in range(size):
            dy = ORDER[start + i] // 16
            from_frame = 2 * ((y + dy) % 2) + from_core
            for j in range(2):
                row = bias[pl.ds(from_frame, 1), pl.ds(2 * samp + j, 1), :].reshape(1, 128)
                biases.append(jnp.concatenate([row] * 4, axis=1))
        both = [
            lax.dot_general(
                keys, q_heads[head], (((1,), (1,)), ((), ())), preferred_element_type=jnp.float32
            ).reshape(size * 2, TOK, 8 * TOK)
            for head in range(2)
        ]
        for head, scores in enumerate(both):
            old = peak[head]
            new = old
            for i in range(size * 2):
                new = jnp.maximum(new, scores[i].max(axis=0, keepdims=True) + biases[i])
            peak[head] = new
            probs = jnp.concatenate(
                [jnp.exp(scores[i] - (new - biases[i])).astype(jnp.bfloat16) for i in range(size * 2)], axis=0
            )
            weighed = jnp.where(top, values_t, one) if head == 0 else jnp.where(top, one, values_t)
            acc[head] = acc[head] * jnp.exp(old - new) + jnp.dot(weighed, probs, preferred_element_type=jnp.float32)

    for group in range(GROUPS):
        mine = kv.at[0, pl.ds(STARTS[group], SIZES[group])]
        theirs = kv.at[1, pl.ds(STARTS[group], SIZES[group])]
        send_next(FLY + 1 + 2 * group)
        wait_bytes(mine, kv_recv.at[group])
        send(mine, theirs, fwd_send, fwd_recv.at[group], sibling, tok)
        work(0, group, core)
        send_next(FLY + 2 + 2 * group)
        wait_bytes(theirs, fwd_recv.at[group])
        work(1, group, 1 - core)

    result = jnp.concatenate(
        [acc[0, :HEAD_DIM] / acc[0, HEAD_DIM:], acc[1, HEAD_DIM:] / acc[1, :HEAD_DIM]], axis=0
    )
    outs[...] = result.T.astype(jnp.bfloat16).reshape(8, TOK, PAIR)
    owner_frame = 2 * y + pair // 4
    for i in range(8):
        column = pl.multiple_of(pair % 4 * PAIR, PAIR)
        send_or_keep(
            outs.at[i], out_ref.at[samp, :, pl.ds(column, PAIR)], out_send, out_recv, owner_frame, 8 * core + i
        )

    wait_bytes(out_ref, out_recv)
    kept = (tok // 8 == core) & (pair // 4 == core)
    wait_sent(outs, out_send, kept)
    wait_sent(q_buf, q_send, kept)
    wait_bytes(others, mask_send)
    for batch in range(len(BATCHES) - FLY, len(BATCHES)):
        wait_batch_sent(batch)
    wait_bytes(kv.at[0], fwd_send)


def body(queries, bank, read_mask):
    return pl.pallas_call(
        kernel,
        out_shape=jax.ShapeDtypeStruct(queries.shape, queries.dtype),
        in_specs=[
            pl.BlockSpec(memory_space=pltpu.HBM),
            pl.BlockSpec(memory_space=pltpu.HBM),
            pl.BlockSpec(memory_space=pltpu.HBM),
        ],
        out_specs=pl.BlockSpec(memory_space=pl.ANY),
        scratch_shapes=[
            pltpu.VMEM((8, TOK, PAIR), jnp.bfloat16),
            pltpu.VMEM((2, 8 * TOK, PAIR), jnp.bfloat16),
            pltpu.VMEM((2, 32, 2, 2, TOK, PAIR), jnp.bfloat16),
            pltpu.VMEM((4, 8, 128), jnp.float32),
            pltpu.VMEM((8, 128), jnp.float32),
            pltpu.SMEM((2, 2), jnp.int32),
            pltpu.VMEM((2, PAIR, 8 * TOK), jnp.float32),
            pltpu.VMEM((2, 1, 8 * TOK), jnp.float32),
            pltpu.VMEM((8, TOK, PAIR), jnp.bfloat16),
            pltpu.SemaphoreType.DMA,
            pltpu.SemaphoreType.DMA,
            pltpu.SemaphoreType.DMA((len(BATCHES),)),
            pltpu.SemaphoreType.DMA((GROUPS,)),
            pltpu.SemaphoreType.DMA,
            pltpu.SemaphoreType.DMA((GROUPS,)),
            pltpu.SemaphoreType.DMA,
            pltpu.SemaphoreType.DMA,
            pltpu.SemaphoreType.DMA,
            pltpu.SemaphoreType.DMA,
            pltpu.SemaphoreType.DMA,
            pltpu.SemaphoreType.REGULAR,
            pltpu.SemaphoreType.REGULAR,
            pltpu.SemaphoreType.REGULAR,
        ],
        compiler_params=pltpu.CompilerParams(
            collective_id=0, has_side_effects=True, vmem_limit_bytes=48 * 1024 * 1024
        ),
    )(queries, bank, read_mask)


def solution(mesh):
    return jax.shard_map(
        body,
        mesh=mesh,
        in_specs=(P("dp", "tok", "frame"), P("dp", "frame", "tok", None), P("dp", "frame")),
        out_specs=P("dp", "tok", "frame"),
        check_vma=False,
    )
```

profile of v0, /device:TPU:1, one launch (start us, length us, event | category | flops | bytes accessed | tf_op | source)
XLA Modules:
  0.0 50.1 jit_solution(12741744459049545044)
XLA Ops:
  0.0 0.0 copy-start
  0.0 1.6 %copy-done = bf16[2,2,64,4096]{3,2,1,0:T(8,128)(2,1)S(1)} copy-done((bf16[2,2,64,4096]{3,2,1,0:T(8,128)(2,1)S(1)}, bf16[2,2,64,4096]{3,2,1,0:T(8,128)(2,1)}, u32[]{:S(2)}) %copy-start) | copy-done | bytes 2097176
  1.6 0.0 copy-start.1
  1.6 0.9 %copy-done.1 = bf16[2,64,512]{2,1,0:T(8,128)(2,1)S(1)} copy-done((bf16[2,64,512]{2,1,0:T(8,128)(2,1)S(1)}, bf16[2,64,512]{2,1,0:T(8,128)(2,1)}, u32[]{:S(2)}) %copy-start.1) | copy-done | bytes 131096
  2.5 0.0 copy-start.2
  2.5 0.7 %copy-done.2 = s32[2,2]{1,0:T(2,128)S(1)} copy-done((s32[2,2]{1,0:T(2,128)S(1)}, s32[2,2]{1,0:T(2,128)}, u32[]{:S(2)}) %copy-start.2) | copy-done | bytes 40
  3.2 46.3 %shard_map.37 = bf16[2,64,512]{2,1,0:T(8,128)(2,1)S(1)} custom-call(bf16[2,64,512]{2,1,0:T(8,128)(2,1)S(1)} %copy-done.1, bf16[2,2,64,4096]{3,2,1,0:T(8,128)(2,1)S(1)} %copy-done, s32[2,2]{1,0:T(2,128)S(1)} %copy-done.2), custom_call_target="tpu_custom_call" | custom-call | tf_op jit(solution)/shard_map/pallas_call | solution.py:212
  49.5 0.7 %copy.5 = bf16[2,64,512]{2,1,0:T(8,128)(2,1)} copy(bf16[2,64,512]{2,1,0:T(8,128)(2,1)S(1)} %shard_map.37) | data formatting | bytes 262144
Async XLA Ops:
  0.0 1.6 %copy-start = (bf16[2,2,64,4096]{3,2,1,0:T(8,128)(2,1)S(1)}, bf16[2,2,64,4096]{3,2,1,0:T(8,128)(2,1)}, u32[]{:S(2)}) copy-start(bf16[2,2,64,4096]{3,2,1,0:T(8,128)(2,1)} %bank_ref.1) | copy-start | bytes 6291460
  1.6 0.9 %copy-start.1 = (bf16[2,64,512]{2,1,0:T(8,128)(2,1)S(1)}, bf16[2,64,512]{2,1,0:T(8,128)(2,1)}, u32[]{:S(2)}) copy-start(bf16[2,64,512]{2,1,0:T(8,128)(2,1)} %q_ref.1) | copy-start | bytes 393220
  2.5 0.7 %copy-start.2 = (s32[2,2]{1,0:T(2,128)S(1)}, s32[2,2]{1,0:T(2,128)}, u32[]{:S(2)}) copy-start(s32[2,2]{1,0:T(2,128)} %mask_ref.1) | copy-start | bytes 52
where the time goes:
time: 50.3 us; the launch traced here: 50.1 us
  Pallas kernels  46.3 us (92%)
  local copies, waits for them, and re-layouts  3.83 us (8%)
    pallas_call x1, Pallas kernels, body(): pl.pallas_call(kernel, out_shape=jax.ShapeDtypeStruct(queries.shape, quer...  46.3 us
    unnamed x7, local copies, waits for them, and re-layouts  3.83 us

commit v1 on v0

--- a/solution.py
+++ b/solution.py
@@ -115,6 +115,9 @@
 
     for mate in x_mates:
         tell(plane_sem, frame, mate)
+    mine_mask, far_mask = bias.at[frame], bias.at[across]
+    send(mask_tile, mine_mask, mask_send.at[0], mask_recv.at[0], across, tok)
+    send(mask_tile, mine_mask, mask_send.at[1], mask_recv.at[1], sibling, tok)
     send_batch(0)
     pl.semaphore_wait(plane_sem, 3)
 
@@ -127,18 +130,17 @@
                 q_ref.at[s, :, pl.ds(j * PAIR, PAIR)], q_buf.at[tok % 8], q_send, q_recv,
                 2 * y + tok // 8, 8 * s + 4 * core + j,
             )
+    wait_bytes(far_mask, mask_recv.at[0])
+    send(far_mask, far_mask, mask_send.at[2], mask_recv.at[2], sibling, tok)
     for batch in range(1, NEAR):
         send_batch(batch)
     pl.semaphore_wait(far_sem, 1)
     for batch in range(NEAR, FLY):
         send_batch(batch)
-    for i in range(1, 4):
-        send(mask_tile, bias.at[frame], mask_send, mask_recv, (frame + i) % 4, tok)
     send_next(FLY)
     wait_bytes(q_buf, q_recv)
-    others = bias.at[pl.ds(0, 3)]
-    wait_bytes(others, mask_recv)
-
+    wait_bytes(mine_mask, mask_recv.at[1])
+    wait_bytes(mine_mask, mask_recv.at[2])
     queries = q_buf[...].reshape(8 * TOK, PAIR).astype(jnp.float32) * (1.0 / math.sqrt(HEAD_DIM))
     first = lax.broadcasted_iota(jnp.int32, queries.shape, 1) < HEAD_DIM
     q_heads[0] = jnp.where(first, queries, 0.0).astype(jnp.bfloat16)
@@ -176,16 +178,25 @@
             weighed = jnp.where(top, values_t, one) if head == 0 else jnp.where(top, one, values_t)
             acc[head] = acc[head] * jnp.exp(old - new) + jnp.dot(weighed, probs, preferred_element_type=jnp.float32)
 
+    def theirs(group):
+        return kv.at[1, pl.ds(STARTS[group], SIZES[group])]
+
+    def work_theirs(group):
+        wait_bytes(theirs(group), fwd_recv.at[group])
+        work(1, group, 1 - core)
+
     for group in range(GROUPS):
         mine = kv.at[0, pl.ds(STARTS[group], SIZES[group])]
-        theirs = kv.at[1, pl.ds(STARTS[group], SIZES[group])]
         send_next(FLY + 1 + 2 * group)
+        send_next(FLY + 2 + 2 * group)
+        if group == GROUPS - 1:
+            work_theirs(group - 1)
         wait_bytes(mine, kv_recv.at[group])
-        send(mine, theirs, fwd_send, fwd_recv.at[group], sibling, tok)
+        send(mine, theirs(group), fwd_send, fwd_recv.at[group], sibling, tok)
         work(0, group, core)
-        send_next(FLY + 2 + 2 * group)
-        wait_bytes(theirs, fwd_recv.at[group])
-        work(1, group, 1 - core)
+        if 0 < group < GROUPS - 1:
+            work_theirs(group - 1)
+    work_theirs(GROUPS - 1)
 
     result = jnp.concatenate(
         [acc[0, :HEAD_DIM] / acc[0, HEAD_DIM:], acc[1, HEAD_DIM:] / acc[1, :HEAD_DIM]], axis=0
@@ -202,7 +213,8 @@
     kept = (tok // 8 == core) & (pair // 4 == core)
     wait_sent(outs, out_send, kept)
     wait_sent(q_buf, q_send, kept)
-    wait_bytes(others, mask_send)
+    for i in range(3):
+        wait_bytes(mask_tile, mask_send.at[i])
     for batch in range(len(BATCHES) - FLY, len(BATCHES)):
         wait_batch_sent(batch)
     wait_bytes(kv.at[0], fwd_send)
@@ -234,8 +246,8 @@
             pltpu.SemaphoreType.DMA((GROUPS,)),
             pltpu.SemaphoreType.DMA,
             pltpu.SemaphoreType.DMA((GROUPS,)),
-            pltpu.SemaphoreType.DMA,
-            pltpu.SemaphoreType.DMA,
+            pltpu.SemaphoreType.DMA((3,)),
+            pltpu.SemaphoreType.DMA((3,)),
             pltpu.SemaphoreType.DMA,
             pltpu.SemaphoreType.DMA,
             pltpu.SemaphoreType.DMA,

time: 50.3 us -> 50.3 us (level)
  no operation moved by 1% of the time
where the time goes in v1:
time: 50.3 us; the launch traced here: 50.2 us
  Pallas kernels  46.3 us (92%)
  local copies, waits for them, and re-layouts  3.83 us (8%)
    pallas_call x1, Pallas kernels, body(): pl.pallas_call(kernel, out_shape=jax.ShapeDtypeStruct(queries.shape, quer...  46.3 us
    unnamed x7, local copies, waits for them, and re-layouts  3.83 us

profile of v1, /device:TPU:1, one launch (start us, length us, event | category | flops | bytes accessed | tf_op | source)
XLA Modules:
  0.0 50.2 jit_solution(11153382377983046)
XLA Ops:
  0.0 0.0 copy-start
  0.0 1.6 %copy-done = bf16[2,2,64,4096]{3,2,1,0:T(8,128)(2,1)S(1)} copy-done((bf16[2,2,64,4096]{3,2,1,0:T(8,128)(2,1)S(1)}, bf16[2,2,64,4096]{3,2,1,0:T(8,128)(2,1)}, u32[]{:S(2)}) %copy-start) | copy-done | bytes 2097176
  1.6 0.0 copy-start.1
  1.6 0.9 %copy-done.1 = bf16[2,64,512]{2,1,0:T(8,128)(2,1)S(1)} copy-done((bf16[2,64,512]{2,1,0:T(8,128)(2,1)S(1)}, bf16[2,64,512]{2,1,0:T(8,128)(2,1)}, u32[]{:S(2)}) %copy-start.1) | copy-done | bytes 131096
  2.5 0.0 copy-start.2
  2.5 0.7 %copy-done.2 = s32[2,2]{1,0:T(2,128)S(1)} copy-done((s32[2,2]{1,0:T(2,128)S(1)}, s32[2,2]{1,0:T(2,128)}, u32[]{:S(2)}) %copy-start.2) | copy-done | bytes 40
  3.2 46.3 %shard_map.37 = bf16[2,64,512]{2,1,0:T(8,128)(2,1)S(1)} custom-call(bf16[2,64,512]{2,1,0:T(8,128)(2,1)S(1)} %copy-done.1, bf16[2,2,64,4096]{3,2,1,0:T(8,128)(2,1)S(1)} %copy-done, s32[2,2]{1,0:T(2,128)S(1)} %copy-done.2), custom_call_target="tpu_custom_call" | custom-call | tf_op jit(solution)/shard_map/pallas_call | solution.py:224
  49.5 0.7 %copy.5 = bf16[2,64,512]{2,1,0:T(8,128)(2,1)} copy(bf16[2,64,512]{2,1,0:T(8,128)(2,1)S(1)} %shard_map.37) | data formatting | bytes 262144
Async XLA Ops:
  0.0 1.6 %copy-start = (bf16[2,2,64,4096]{3,2,1,0:T(8,128)(2,1)S(1)}, bf16[2,2,64,4096]{3,2,1,0:T(8,128)(2,1)}, u32[]{:S(2)}) copy-start(bf16[2,2,64,4096]{3,2,1,0:T(8,128)(2,1)} %bank_ref.1) | copy-start | bytes 6291460
  1.6 0.9 %copy-start.1 = (bf16[2,64,512]{2,1,0:T(8,128)(2,1)S(1)}, bf16[2,64,512]{2,1,0:T(8,128)(2,1)}, u32[]{:S(2)}) copy-start(bf16[2,64,512]{2,1,0:T(8,128)(2,1)} %q_ref.1) | copy-start | bytes 393220
  2.5 0.7 %copy-start.2 = (s32[2,2]{1,0:T(2,128)S(1)}, s32[2,2]{1,0:T(2,128)}, u32[]{:S(2)}) copy-start(s32[2,2]{1,0:T(2,128)} %mask_ref.1) | copy-start | bytes 52
